TPU v7x, 32 devices: a whole 2x2x4 slice. The times are simulated.
32 devices in a mesh: row: 4 (over z), col: 4 (over y, x), pair: 2 (over core).
Axes of the slice: x: 2, y: 2, z: 4, core: 2. Of those that a mesh axis runs over, the one named last changes fastest.
Arguments:
- integrals: bfloat16 [2048, 2048], P('row', ('col', 'pair')), may hold values from -0.1875 to 0.1875
- int_mask: int32 [32, 32], P('row', ('col', 'pair')), may hold values 0 or 1
- amplitudes: bfloat16 [2048, 2048], P('row', ('col', 'pair')), may hold values from -6 to 6
- domain_mask: int32 [32, 2048], P('row', ('col', 'pair')), may hold values 0 or 1
- virt_energy: float32 [2048], P('row'), may hold values from 0.5 to 4
- occ_energy: float32 [2048], P(('col', 'pair')), may hold values from -3 to -0.5
Outputs:
- update: float32 [2048, 2048], P('row', ('col', 'pair'))
All inputs are finite; a program needn't handle non-finite values. No bound on the sum of `int_mask` or of `domain_mask` on one device may be relied on, other than what follows from the above.
Results may differ from a plain program's by a relative error of at most 0.0003.
Values may be sent and summed in bfloat16 or wider, within the bound.
A program may use at most 64 MiB of HBM per device.

v0:
```python
import functools

import jax
import jax.numpy as jnp
from jax import lax
from jax.experimental import pallas as pl
from jax.experimental.pallas import tpu as pltpu
from jax.sharding import PartitionSpec as P

TILE = 64
PIECES = 1
MESH = pl.DeviceIdType.MESH


def flipped(index, distance, count):
    out, bit = 0, 1
    while bit < count:
        have = lax.rem(index // bit, 2)
        out = out + bit * (1 - have if (distance // bit) % 2 else have)
        bit *= 2
    return out


def kernel(R, C, a_hbm, im_hbm, b_hbm, dm_hbm, v_hbm, o_hbm, out_ref,
           a_all, b_all, acc, inv, im_ref, dm_ref, v_ref, o_ref, load_sem, store_sem,
           a_send, a_recv, sib_send, sib_recv, dn_send, dn_recv, up_send, up_recv):
    r, c, p = lax.axis_index("row"), lax.axis_index("col"), lax.axis_index("pair")
    q = 1 - p
    me = c * 2 + p
    rows, width = a_hbm.shape
    depth, cols = b_hbm.shape
    parts = depth // width
    half = rows // 2
    bits = [1 << i for i in range(C.bit_length() - 1)]

    loads = [
        pltpu.make_async_copy(src, dst, load_sem.at[i]) for i, (src, dst) in enumerate([
            (dm_hbm, dm_ref), (b_hbm, b_all.at[r]), (im_hbm, im_ref), (a_hbm, a_all.at[me]),
            (v_hbm, v_ref), (o_hbm, o_ref)])
    ]
    for load in loads:
        load.start()

    others = [flipped(c, d, C) for d in range(C)]
    barrier = pltpu.get_barrier_semaphore()

    def greet(device):
        pl.semaphore_signal(barrier, inc=1, device_id=device, device_id_type=MESH)

    greet((r, c, q))
    for e in bits:
        greet((r, others[e], p))

    @pl.when(r > 0)
    def _():
        greet((r - 1, c, p))

    @pl.when(r < R - 1)
    def _():
        greet((r + 1, c, p))

    def part(block, j):
        return b_all.at[block, pl.ds(j * width, width)]

    def down(block, s, j):
        return pltpu.make_async_remote_copy(
            src_ref=part(block, j), dst_ref=part(block, j),
            send_sem=dn_send.at[s, j], recv_sem=dn_recv.at[s, j],
            device_id=(r - 1, c, p), device_id_type=MESH)

    def up(block, s, j):
        return pltpu.make_async_remote_copy(
            src_ref=part(block, j), dst_ref=part(block, j),
            send_sem=up_send.at[s, j], recv_sem=up_recv.at[s, j],
            device_id=(r + 1, c, p), device_id_type=MESH)

    def across(d, e, h):
        piece = a_all.at[others[d] * 2 + p, pl.ds(h * half, half)]
        return pltpu.make_async_remote_copy(
            src_ref=piece, dst_ref=piece,
            send_sem=a_send.at[d + e, h], recv_sem=a_recv.at[d + e, h],
            device_id=(r, others[e], p), device_id_type=MESH)

    def sibling(d, h, core=None):
        piece = a_all.at[others[d] * 2 + (p if core is None else core), pl.ds(h * half, half)]
        return pltpu.make_async_remote_copy(
            src_ref=piece, dst_ref=piece,
            send_sem=sib_send.at[d, h], recv_sem=sib_recv.at[d, h],
            device_id=(r, c, q), device_id_type=MESH)

    def onward(d, h):
        if d == 0:
            return bits
        low, high = d & -d, 1 << (d.bit_length() - 1)
        return [e for e in bits if (e < low if h == 0 else e > high)]

    def arrives(d, h):
        low, high = d & -d, 1 << (d.bit_length() - 1)
        e = low if h == 0 else high
        piece = a_all.at[others[d] * 2 + p, pl.ds(h * half, half)]
        pltpu.make_async_remote_copy(
            src_ref=piece, dst_ref=piece,
            send_sem=a_send.at[d, h], recv_sem=a_recv.at[d, h],
            device_id=(r, others[e], p), device_id_type=MESH).wait_recv()
        for e in onward(d, h):
            across(d, e, h).start()
        sibling(d, h).start()

    loads[0].wait()
    loads[1].wait()
    for t in range(depth // TILE):
        keep = dm_ref[t:t + 1, :].astype(jnp.bfloat16)
        here = pl.ds(t * TILE, TILE)
        b_all[r, here, :] = b_all[r, here, :] * keep

    pl.semaphore_wait(barrier, 1 + len(bits) + (r + R - 1) // R + (2 * R - 2 - r) // R)

    for j in range(parts):
        @pl.when(r > 0)
        def _():
            down(r, 0, j).start()

        @pl.when(r < R - 1)
        def _():
            up(r, 0, j).start()

    loads[2].wait()
    loads[3].wait()
    lane = lax.broadcasted_iota(jnp.int32, (1, width), 1) // TILE
    for t in range(rows // TILE):
        keep = jnp.zeros((1, width), jnp.float32)
        for u in range(width // TILE):
            keep = jnp.where(lane == u, im_ref[u:u + 1, t:t + 1].astype(jnp.float32), keep)
        here = pl.ds(t * TILE, TILE)
        a_all[me, here, :] = a_all[me, here, :] * keep.astype(jnp.bfloat16)

    for h in (1, 0):
        for e in bits:
            g = h if 2 * e < C else 1 - h
            across(0, e, g).start()
    for h in range(2):
        sibling(0, h).start()

    loads[4].wait()
    loads[5].wait()
    for t in range(rows // 128):
        v = jnp.broadcast_to(v_ref[:, t * 128:(t + 1) * 128], (128, 128)).T
        for u in range(cols // 128):
            lanes = slice(u * 128, (u + 1) * 128)
            factor = 1.0 / (v - o_ref[:, lanes])
            for w in range(128 // TILE):
                row = t * (128 // TILE) + w
                keep = dm_ref[row:row + 1, lanes].astype(jnp.float32)
                inv[pl.ds(row * TILE, TILE), lanes] = factor[w * TILE:(w + 1) * TILE] * keep

    def receive(s, j):
        above, below = r + s + 1, r - s - 1

        @pl.when(above < R)
        def _():
            down(above, s, j).wait_recv()

            @pl.when(r > 0)
            def _():
                down(above, s + 1, j).start()

        @pl.when(below >= 0)
        def _():
            up(below, s, j).wait_recv()

            @pl.when(r < R - 1)
            def _():
                up(below, s + 1, j).start()

    whole = pl.ds(0, rows)

    def product(block, j, here=whole):
        return jnp.dot(a_all[block * parts + j, here, :], b_all[block, j * width:(j + 1) * width],
                       preferred_element_type=jnp.float32)

    def add(s, j, here=whole):
        @pl.when(r + s + 1 < R)
        def _():
            acc[here, :] += product(r + s + 1, j, here)

        @pl.when(r - s - 1 >= 0)
        def _():
            acc[here, :] += product(r - s - 1, j, here)

    along = [(0, j) for j in range(parts)]
    near = [d for d in range(1, C) if d in bits]
    for h in (1, 0):
        for d in near:
            arrives(d, h if 2 * d < C else 1 - h)
        if along:
            receive(*along.pop(0))
    while along:
        receive(*along.pop(0))
    for d in sorted(range(1, C), key=lambda d: d.bit_count()):
        if d not in near:
            for h in range(2):
                arrives(d, h)
    later = [(s, j) for s in range(1, R - 1) for j in range(parts)]
    if later:
        receive(*later[0])
    for d in range(C):
        for h in range(2):
            sibling(d, h, q).wait_recv()

    acc[...] = product(r, 0)
    for j in range(1, parts):
        acc[...] += product(r, j)
    due = [(0, j) for j in range(parts)]
    for item in later[:1]:
        add(*due.pop(0))
        due.append(item)
    for item in later[1:]:
        if item == later[-1]:
            while due:
                add(*due.pop(0))
        receive(*item)
        due.append(item)
        if item != later[-1]:
            add(*due.pop(0))

    stores = []
    for t in range(PIECES):
        here = pl.ds(t * (rows // PIECES), rows // PIECES)
        for s, j in due:
            add(s, j, here)
        acc[here, :] = acc[here, :] * inv[here, :]
        stores.append(pltpu.make_async_copy(acc.at[here], out_ref.at[here], store_sem.at[t]))
        stores[-1].start()

    for d in range(C):
        for h in range(2):
            sibling(d, h).wait_send()
            for e in onward(d, h):
                across(d, e, h).wait_send()
    for s in range(R - 1):
        for j in range(parts):
            @pl.when((r + s < R) & (r > 0))
            def _():
                down(r + s, s, j).wait_send()

            @pl.when((r - s >= 0) & (r < R - 1))
            def _():
                up(r - s, s, j).wait_send()
    for store in stores:
        store.wait()


def solution(mesh):
    R, C = mesh.shape["row"], mesh.shape["col"]

    def local(integrals, int_mask, amplitudes, domain_mask, virt_energy, occ_energy):
        rows, width = integrals.shape
        depth, cols = amplitudes.shape
        parts = depth // width
        hbm = pl.BlockSpec(memory_space=pl.ANY)
        dma = pltpu.SemaphoreType.DMA
        return pl.pallas_call(
            functools.partial(kernel, R, C),
            out_shape=jax.ShapeDtypeStruct((rows, cols), jnp.float32),
            in_specs=[hbm] * 6,
            out_specs=hbm,
            scratch_shapes=[
                pltpu.VMEM((C * 2, rows, width), jnp.bfloat16),
                pltpu.VMEM((R, depth, cols), jnp.bfloat16),
                pltpu.VMEM((rows, cols), jnp.float32),
                pltpu.VMEM((rows, cols), jnp.float32),
                pltpu.VMEM(int_mask.shape[::-1], jnp.int32),
                pltpu.VMEM(domain_mask.shape, jnp.int32),
                pltpu.VMEM((1, rows), jnp.float32),
                pltpu.VMEM((1, cols), jnp.float32),
                dma((6,)), dma((PIECES,)), dma((C, 2)), dma((C, 2)), dma((C, 2)), dma((C, 2)),
                dma((R - 1, parts)), dma((R - 1, parts)), dma((R - 1, parts)), dma((R - 1, parts)),
            ],
            compiler_params=pltpu.CompilerParams(
                collective_id=0, has_side_effects=True, vmem_limit_bytes=62 * 2**20),
            cost_estimate=pl.CostEstimate(
                flops=2 * rows * depth * R * cols, bytes_accessed=4 * 2**20, transcendentals=0),
        )(integrals, int_mask.T, amplitudes, domain_mask,
          virt_energy.reshape(1, rows), occ_energy.reshape(1, cols))

    placed = (
        P("row", ("col", "pair")),
        P("row", ("col", "pair")),
        P("row", ("col", "pair")),
        P("row", ("col", "pair")),
        P("row"),
        P(("col", "pair")),
    )
    return jax.shard_map(
        local, mesh=mesh, in_specs=placed, out_specs=P("row", ("col", "pair")), check_vma=False
    )
```

profile of v0, /device:TPU:0, one launch (start us, length us, event | category | flops | bytes accessed | tf_op | source)
XLA Modules:
  0.0 25.7 jit_solution(9616926377465914872)
XLA Ops:
  0.0 23.8 %shard_map.64 = f32[512,256]{1,0:T(8,128)} custom-call(bf16[512,256]{1,0:T(8,128)(2,1)} %a_hbm.1, s32[4,8]{1,0:T(4,128)} %bitcast.3, bf16[512,256]{1,0:T(8,128)(2,1)} %b_hbm.1, s32[8,256]{1,0:T(8,128)} %dm_hbm.1, f32[1,512]{1,0:T(1,128)} %bitcast.4, f32[1,256]{1,0:T(1,128)} %bitcast.5), custom_call_target="tpu_custom_call" | custom-call | flops 536870912 | bytes 4194304 | tf_op jit(solution)/shard_map/pallas_call | solution.py:262
  23.8 1.9 %copy.8 = f32[512,256]{1,0:T(8,128)} copy(f32[512,256]{1,0:T(8,128)} %shard_map.64) | data formatting | bytes 1048576
where the time goes:
time: 25.9 us; the launch traced here: 25.7 us
  Pallas kernels  23.8 us (92%)
  local copies, waits for them, and re-layouts  1.87 us (7%)
    pallas_call x1, Pallas kernels, local(): pl.pallas_call(functools.partial(kernel, R, C), out_shape=jax.ShapeDtypeS...  23.8 us
    unnamed x1, local copies, waits for them, and re-layouts  1.87 us

commit v1 on v0

--- a/solution.py
+++ b/solution.py
@@ -229,8 +229,7 @@
         for s, j in due:
             add(s, j, here)
         acc[here, :] = acc[here, :] * inv[here, :]
-        stores.append(pltpu.make_async_copy(acc.at[here], out_ref.at[here], store_sem.at[t]))
-        stores[-1].start()
+        out_ref[here, :] = acc[here, :]
 
     for d in range(C):
         for h in range(2):
@@ -261,9 +260,9 @@
         dma = pltpu.SemaphoreType.DMA
         return pl.pallas_call(
             functools.partial(kernel, R, C),
-            out_shape=jax.ShapeDtypeStruct((rows, cols), jnp.float32),
+            out_shape=pltpu.VMEM((rows, cols), jnp.float32),
             in_specs=[hbm] * 6,
-            out_specs=hbm,
+            out_specs=pl.BlockSpec(memory_space=pltpu.VMEM),
             scratch_shapes=[
                 pltpu.VMEM((C * 2, rows, width), jnp.bfloat16),
                 pltpu.VMEM((R, depth, cols), jnp.bfloat16),
@@ -277,11 +276,11 @@
                 dma((R - 1, parts)), dma((R - 1, parts)), dma((R - 1, parts)), dma((R - 1, parts)),
             ],
             compiler_params=pltpu.CompilerParams(
-                collective_id=0, has_side_effects=True, vmem_limit_bytes=62 * 2**20),
+                collective_id=0, has_side_effects=True, vmem_limit_bytes=32 * 2**20),
             cost_estimate=pl.CostEstimate(
                 flops=2 * rows * depth * R * cols, bytes_accessed=4 * 2**20, transcendentals=0),
-        )(integrals, int_mask.T, amplitudes, domain_mask,
-          virt_energy.reshape(1, rows), occ_energy.reshape(1, cols))
+        )(*[pltpu.with_memory_space_constraint(z, pltpu.HBM) for z in (integrals, int_mask.T, amplitudes, domain_mask,
+          virt_energy.reshape(1, rows), occ_energy.reshape(1, cols))])
 
     placed = (
         P("row", ("col", "pair")),

time: 25.9 us -> 24.1 us (0.931)
  local copies, waits for them, and re-layouts: 1.87 us -> 0.8 us
  Pallas kernels: 23.8 us -> 23.1 us
    unnamed x1, local copies, waits for them, and re-layouts: 1.87 us -> 0.8 us
    pallas_call x1, Pallas kernels: 23.8 us -> 23.1 us  [local(): pl.pallas_call(functools.partial(kernel, R, C), out_shape=pltpu.VMEM((row...]
where the time goes in v1:
time: 24.1 us; the launch traced here: 23.9 us
  Pallas kernels  23.1 us (96%)
  local copies, waits for them, and re-layouts  0.8 us (3%)
    pallas_call x1, Pallas kernels, local(): pl.pallas_call(functools.partial(kernel, R, C), out_shape=pltpu.VMEM((row...  23.1 us
    unnamed x1, local copies, waits for them, and re-layouts  0.8 us

profile of v1, /device:TPU:0, one launch (start us, length us, event | category | flops | bytes accessed | tf_op | source)
XLA Modules:
  0.0 23.9 jit_solution(14915544918969538948)
XLA Ops:
  0.0 23.1 %shard_map.64 = f32[512,256]{1,0:T(8,128)S(1)} custom-call(bf16[512,256]{1,0:T(8,128)(2,1)} %a_hbm.1, s32[4,8]{1,0:T(4,128)} %bitcast.3, bf16[512,256]{1,0:T(8,128)(2,1)} %b_hbm.1, s32[8,256]{1,0:T(8,128)} %dm_hbm.1, f32[1,512]{1,0:T(1,128)} %bitcast.4, f32[1,256]{1,0:T(1,128)} %bitcast.5), custom_call_target="tpu_custom_call" | custom-call | flops 536870912 | bytes 4194304 | tf_op jit(solution)/shard_map/pallas_call | solution.py:261
  23.1 0.8 %copy.8 = f32[512,256]{1,0:T(8,128)} copy(f32[512,256]{1,0:T(8,128)S(1)} %shard_map.64) | data formatting | bytes 1048576

commit v2 on v1

v2 whole, which is shorter than its diff:
```python
import functools

import jax
import jax.numpy as jnp
from jax import lax
from jax.experimental import pallas as pl
from jax.experimental.pallas import tpu as pltpu
from jax.sharding import PartitionSpec as P

TILE = 64
SPLIT = 2
MESH = pl.DeviceIdType.MESH


def flipped(index, distance, count):
    out, bit = 0, 1
    while bit < count:
        have = lax.rem(index // bit, 2)
        out = out + bit * (1 - have if (distance // bit) % 2 else have)
        bit *= 2
    return out


def kernel(R, C, a_hbm, im_hbm, b_hbm, dm_hbm, v_hbm, o_hbm, acc,
           a_all, b_all, inv, im_ref, dm_ref, dm_above, v_ref, o_ref, load_sem,
           a_send, a_recv, sib_send, sib_recv, dn_send, dn_recv, up_send, up_recv, dm_send, dm_recv,
           above_in, plane_in, go):
    r, c, p = lax.axis_index("row"), lax.axis_index("col"), lax.axis_index("pair")
    q = 1 - p
    me = c * 2 + p
    rows, width = a_hbm.shape
    depth, cols = b_hbm.shape
    parts = depth // width
    pieces = parts * SPLIT
    tall = depth // pieces
    half = rows // 2
    bits = [1 << i for i in range(C.bit_length() - 1)]
    others = [flipped(c, d, C) for d in range(C)]

    loads = [
        pltpu.make_async_copy(src, dst, load_sem.at[i]) for i, (src, dst) in enumerate([
            (dm_hbm, dm_ref), (b_hbm, b_all.at[r]), (im_hbm, im_ref), (a_hbm, a_all.at[me]),
            (v_hbm, v_ref), (o_hbm, o_ref)])
    ]

    barrier = pltpu.get_barrier_semaphore()

    def greet(device):
        pl.semaphore_signal(barrier, inc=1, device_id=device, device_id_type=MESH)

    @pl.when(r < R - 1)
    def _():
        greet((r + 1, c, p))

    @pl.when(p == 1)
    def _():
        for e in bits:
            greet((r, others[e], p))

        @pl.when(r > 0)
        def _():
            greet((r - 1, c, p))

    @pl.when(p == 0)
    def _():
        greet((r, c, q))

    for load in loads:
        load.start()

    @pl.when(p == 1)
    def _():
        pl.semaphore_wait(barrier, (r + R - 1) // R + (2 * R - 2 - r) // R + len(bits) + 1)

    @pl.when((p == 0) & (r > 0))
    def _():
        pl.semaphore_wait(barrier, 1)
        pl.semaphore_signal(above_in, inc=1, device_id=(r - 1, c, p), device_id_type=MESH)

    @pl.when(p == 1)
    def _():
        for e in bits:
            pl.semaphore_signal(plane_in, inc=1, device_id=(r, others[e], p), device_id_type=MESH)

    def strip(block, j):
        return b_all.at[block, pl.ds(j * tall, tall)]

    def down(block, s, j):
        return pltpu.make_async_remote_copy(
            src_ref=strip(block, j), dst_ref=strip(block, j),
            send_sem=dn_send.at[s, j], recv_sem=dn_recv.at[s, j],
            device_id=(r - 1, c, p), device_id_type=MESH)

    def up(block, s, j):
        return pltpu.make_async_remote_copy(
            src_ref=strip(block, j), dst_ref=strip(block, j),
            send_sem=up_send.at[s, j], recv_sem=up_recv.at[s, j],
            device_id=(r + 1, c, p), device_id_type=MESH)

    def raw(j):
        return pltpu.make_async_remote_copy(
            src_ref=b_hbm.at[pl.ds(j * tall, tall)], dst_ref=strip(r, j),
            send_sem=dn_send.at[0, j], recv_sem=dn_recv.at[0, j],
            device_id=(r - 1, c, p), device_id_type=MESH)

    def domains():
        return pltpu.make_async_remote_copy(
            src_ref=dm_hbm, dst_ref=dm_above, send_sem=dm_send, recv_sem=dm_recv,
            device_id=(r - 1, c, p), device_id_type=MESH)

    def across(d, e, h):
        piece = a_all.at[others[d] * 2 + p, pl.ds(h * half, half)]
        return pltpu.make_async_remote_copy(
            src_ref=piece, dst_ref=piece,
            send_sem=a_send.at[d + e, h], recv_sem=a_recv.at[d + e, h],
            device_id=(r, others[e], p), device_id_type=MESH)

    def sibling(d, h, core=None):
        piece = a_all.at[others[d] * 2 + (p if core is None else core), pl.ds(h * half, half)]
        return pltpu.make_async_remote_copy(
            src_ref=piece, dst_ref=piece,
            send_sem=sib_send.at[d, h], recv_sem=sib_recv.at[d, h],
            device_id=(r, c, q), device_id_type=MESH)

    def onward(d, h):
        if d == 0:
            return bits
        low, high = d & -d, 1 << (d.bit_length() - 1)
        return [e for e in bits if (e < low if h == 0 else e > high)]

    def arrives(d, h):
        low, high = d & -d, 1 << (d.bit_length() - 1)
        e = low if h == 0 else high
        piece = a_all.at[others[d] * 2 + p, pl.ds(h * half, half)]
        pltpu.make_async_remote_copy(
            src_ref=piece, dst_ref=piece,
            send_sem=a_send.at[d, h], recv_sem=a_recv.at[d, h],
            device_id=(r, others[e], p), device_id_type=MESH).wait_recv()
        for e in onward(d, h):
            across(d, e, h).start()
        sibling(d, h).start()

    def mask(block, j, domain):
        for t in range(j * tall // TILE, (j + 1) * tall // TILE):
            here = pl.ds(t * TILE, TILE)
            b_all[block, here, :] = b_all[block, here, :] * domain[t:t + 1, :].astype(jnp.bfloat16)

    @pl.when(r == 1)
    def _():
        raw(0).start()
        domains().start()
        for j in range(1, pieces):
            raw(j).start()

    loads[0].wait()
    loads[1].wait()
    for j in range(pieces):
        mask(r, j, dm_ref)

        @pl.when(r > 1)
        def _():
            down(r, 0, j).start()

    @pl.when((p == 0) & (r < R - 1))
    def _():
        pl.semaphore_wait(above_in, 1)

    @pl.when(r < R - 1)
    def _():
        for j in range(pieces):
            up(r, 0, j).start()

    @pl.when(p == 1)
    def _():
        pl.semaphore_wait(plane_in, len(bits))
        pl.semaphore_signal(go, inc=1, device_id=(r, c, q), device_id_type=MESH)

    loads[2].wait()
    loads[3].wait()
    lane = lax.broadcasted_iota(jnp.int32, (1, width), 1) // TILE
    for t in range(rows // TILE):
        keep = jnp.zeros((1, width), jnp.float32)
        for u in range(width // TILE):
            keep = jnp.where(lane == u, im_ref[u:u + 1, t:t + 1].astype(jnp.float32), keep)
        here = pl.ds(t * TILE, TILE)
        a_all[me, here, :] = a_all[me, here, :] * keep.astype(jnp.bfloat16)

    @pl.when(p == 0)
    def _():
        pl.semaphore_wait(go, 1)

    for h in (1, 0):
        for e in bits:
            g = h if 2 * e < C else 1 - h
            across(0, e, g).start()
    for h in range(2):
        sibling(0, h).start()

    loads[4].wait()
    loads[5].wait()
    for t in range(rows // 128):
        v = jnp.broadcast_to(v_ref[:, t * 128:(t + 1) * 128], (128, 128)).T
        for u in range(cols // 128):
            lanes = slice(u * 128, (u + 1) * 128)
            factor = 1.0 / (v - o_ref[:, lanes])
            for w in range(128 // TILE):
                row = t * (128 // TILE) + w
                keep = dm_ref[row:row + 1, lanes].astype(jnp.float32)
                inv[pl.ds(row * TILE, TILE), lanes] = factor[w * TILE:(w + 1) * TILE] * keep

    def receive(s, j):
        above, below = r + s + 1, r - s - 1

        @pl.when(above < R)
        def _():
            down(above, s, j).wait_recv()

            @pl.when(r > 0)
            def _():
                down(above, s + 1, j).start()

            if s == 0:
                @pl.when(r == 0)
                def _():
                    if j == 0:
                        domains().wait_recv()
                    mask(1, j, dm_above)

        @pl.when(below >= 0)
        def _():
            up(below, s, j).wait_recv()

            @pl.when(r < R - 1)
            def _():
                up(below, s + 1, j).start()

    def product(block, j, part=0, of=1):
        deep = width // of
        k = pl.ds(j * width + part * deep, deep)
        return jnp.dot(a_all[block * parts + j, :, part * deep:(part + 1) * deep], b_all[block, k, :],
                       preferred_element_type=jnp.float32)

    def add(s, j):
        @pl.when(r + s + 1 < R)
        def _():
            acc[...] += product(r + s + 1, j)

        @pl.when(r - s - 1 >= 0)
        def _():
            acc[...] += product(r - s - 1, j)

    strips = [(s, j) for s in range(R - 1) for j in range(pieces)]

    def take(count):
        for _ in range(count):
            if len(strips) > SPLIT:
                receive(*strips.pop(0))

    near = [d for d in range(1, C) if d in bits]
    take(2)
    for h in (1, 0):
        for d in near:
            arrives(d, h if 2 * d < C else 1 - h)
        take(2)
    for d in sorted(range(1, C), key=lambda d: d.bit_count()):
        if d not in near:
            for h in range(2):
                arrives(d, h)
    take(1)
    for d in range(C):
        for h in range(2):
            sibling(d, h, q).wait_recv()

    acc[...] = product(r, 0)
    for j in range(1, parts):
        acc[...] += product(r, j)
    whole = [(s, j) for s in range(R - 1) for j in range(parts)]
    for s, j in whole[:-1]:
        while strips and strips[0] <= (s, (j + 1) * SPLIT - 1):
            receive(*strips.pop(0))
        add(s, j)

    s, j = whole[-1]
    for i in range(SPLIT - 1):
        receive(s, j * SPLIT + i)

        @pl.when(r == 0)
        def _():
            acc[...] += product(R - 1, j, i, SPLIT)

        @pl.when(r == R - 1)
        def _():
            acc[...] += product(0, j, i, SPLIT)

    receive(s, pieces - 1)

    @pl.when(r == 0)
    def _():
        acc[...] = (acc[...] + product(R - 1, j, SPLIT - 1, SPLIT)) * inv[...]

    @pl.when(r == R - 1)
    def _():
        acc[...] = (acc[...] + product(0, j, SPLIT - 1, SPLIT)) * inv[...]

    @pl.when((r > 0) & (r < R - 1))
    def _():
        acc[...] = acc[...] * inv[...]

    for d in range(C):
        for h in range(2):
            sibling(d, h).wait_send()
            for e in onward(d, h):
                across(d, e, h).wait_send()
    for s in range(R - 1):
        for j in range(pieces):
            @pl.when((r + s < R) & (r > 0))
            def _():
                down(r + s, s, j).wait_send()

            @pl.when((r - s >= 0) & (r < R - 1))
            def _():
                up(r - s, s, j).wait_send()

    @pl.when(r == 1)
    def _():
        domains().wait_send()


def solution(mesh):
    R, C = mesh.shape["row"], mesh.shape["col"]

    def local(integrals, int_mask, amplitudes, domain_mask, virt_energy, occ_energy):
        rows, width = integrals.shape
        depth, cols = amplitudes.shape
        pieces = depth // width * SPLIT
        hbm = pl.BlockSpec(memory_space=pl.ANY)
        dma = pltpu.SemaphoreType.DMA
        operands = (integrals, int_mask.T, amplitudes, domain_mask,
                    virt_energy.reshape(1, rows), occ_energy.reshape(1, cols))
        return pl.pallas_call(
            functools.partial(kernel, R, C),
            out_shape=pltpu.VMEM((rows, cols), jnp.float32),
            in_specs=[hbm] * 6,
            out_specs=pl.BlockSpec(memory_space=pltpu.VMEM),
            scratch_shapes=[
                pltpu.VMEM((C * 2, rows, width), jnp.bfloat16),
                pltpu.VMEM((R, depth, cols), jnp.bfloat16),
                pltpu.VMEM((rows, cols), jnp.float32),
                pltpu.VMEM(int_mask.shape[::-1], jnp.int32),
                pltpu.VMEM(domain_mask.shape, jnp.int32),
                pltpu.VMEM(domain_mask.shape, jnp.int32),
                pltpu.VMEM((1, rows), jnp.float32),
                pltpu.VMEM((1, cols), jnp.float32),
                dma((6,)), dma((C, 2)), dma((C, 2)), dma((C, 2)), dma((C, 2)),
                dma((R - 1, pieces)), dma((R - 1, pieces)), dma((R - 1, pieces)), dma((R - 1, pieces)),
                dma, dma,
                pltpu.SemaphoreType.REGULAR, pltpu.SemaphoreType.REGULAR, pltpu.SemaphoreType.REGULAR,
            ],
            compiler_params=pltpu.CompilerParams(
                collective_id=0, has_side_effects=True, vmem_limit_bytes=32 * 2**20),
            cost_estimate=pl.CostEstimate(
                flops=2 * rows * depth * R * cols, bytes_accessed=4 * 2**20, transcendentals=0),
        )(*[pltpu.with_memory_space_constraint(x, pltpu.HBM) for x in operands])

    placed = (
        P("row", ("col", "pair")),
        P("row", ("col", "pair")),
        P("row", ("col", "pair")),
        P("row", ("col", "pair")),
        P("row"),
        P(("col", "pair")),
    )
    return jax.shard_map(
        local, mesh=mesh, in_specs=placed, out_specs=P("row", ("col", "pair")), check_vma=False
    )
```

time: 24.1 us -> 23.6 us (0.979)
  Pallas kernels: 23.1 us -> 22.6 us
    pallas_call x1, Pallas kernels: 23.1 us -> 22.6 us  [local(): pl.pallas_call(functools.partial(kernel, R, C), out_shape=pltpu.VMEM((row...]
where the time goes in v2:
time: 23.6 us; the launch traced here: 23.4 us
  Pallas kernels  22.6 us (96%)
  local copies, waits for them, and re-layouts  0.8 us (3%)
    pallas_call x1, Pallas kernels, local(): pl.pallas_call(functools.partial(kernel, R, C), out_shape=pltpu.VMEM((row...  22.6 us
    unnamed x1, local copies, waits for them, and re-layouts  0.8 us

profile of v2, /device:TPU:0, one launch (start us, length us, event | category | flops | bytes accessed | tf_op | source)
XLA Modules:
  0.0 23.4 jit_solution(65345781147855096)
XLA Ops:
  0.0 22.6 %shard_map.64 = f32[512,256]{1,0:T(8,128)S(1)} custom-call(bf16[512,256]{1,0:T(8,128)(2,1)} %a_hbm.1, s32[4,8]{1,0:T(4,128)} %bitcast.3, bf16[512,256]{1,0:T(8,128)(2,1)} %b_hbm.1, s32[8,256]{1,0:T(8,128)} %dm_hbm.1, f32[1,512]{1,0:T(1,128)} %bitcast.4, f32[1,256]{1,0:T(1,128)} %bitcast.5), custom_call_target="tpu_custom_call" | custom-call | flops 536870912 | bytes 4194304 | tf_op jit(solution)/shard_map/pallas_call | solution.py:340
  22.6 0.8 %copy.8 = f32[512,256]{1,0:T(8,128)} copy(f32[512,256]{1,0:T(8,128)S(1)} %shard_map.64) | data formatting | bytes 1048576

commit v3 on v2

--- a/solution.py
+++ b/solution.py
@@ -9,6 +9,9 @@
 
 TILE = 64
 SPLIT = 2
+FIRST = 1
+LENT = 64
+HELPER = 3
 MESH = pl.DeviceIdType.MESH
 
 
@@ -24,7 +27,7 @@
 def kernel(R, C, a_hbm, im_hbm, b_hbm, dm_hbm, v_hbm, o_hbm, acc,
            a_all, b_all, inv, im_ref, dm_ref, dm_above, v_ref, o_ref, load_sem,
            a_send, a_recv, sib_send, sib_recv, dn_send, dn_recv, up_send, up_recv, dm_send, dm_recv,
-           above_in, plane_in, go):
+           lent, lend_send, lend_recv, pass_send, pass_recv, above_in, plane_in, go):
     r, c, p = lax.axis_index("row"), lax.axis_index("col"), lax.axis_index("pair")
     q = 1 - p
     me = c * 2 + p
@@ -36,6 +39,9 @@
     half = rows // 2
     bits = [1 << i for i in range(C.bit_length() - 1)]
     others = [flipped(c, d, C) for d in range(C)]
+    first = depth - LENT
+    giver, taker = (r == 1) & (c == 0), (r == 0) & (c == 0)
+    helper = (r == 1) & (c == HELPER) & (p == 1)
 
     loads = [
         pltpu.make_async_copy(src, dst, load_sem.at[i]) for i, (src, dst) in enumerate([
@@ -57,10 +63,6 @@
         for e in bits:
             greet((r, others[e], p))
 
-        @pl.when(r > 0)
-        def _():
-            greet((r - 1, c, p))
-
     @pl.when(p == 0)
     def _():
         greet((r, c, q))
@@ -70,17 +72,11 @@
 
     @pl.when(p == 1)
     def _():
-        pl.semaphore_wait(barrier, (r + R - 1) // R + (2 * R - 2 - r) // R + len(bits) + 1)
+        pl.semaphore_wait(barrier, (r + R - 1) // R + len(bits) + 1)
 
     @pl.when((p == 0) & (r > 0))
     def _():
         pl.semaphore_wait(barrier, 1)
-        pl.semaphore_signal(above_in, inc=1, device_id=(r - 1, c, p), device_id_type=MESH)
-
-    @pl.when(p == 1)
-    def _():
-        for e in bits:
-            pl.semaphore_signal(plane_in, inc=1, device_id=(r, others[e], p), device_id_type=MESH)
 
     def strip(block, j):
         return b_all.at[block, pl.ds(j * tall, tall)]
@@ -102,6 +98,25 @@
             src_ref=b_hbm.at[pl.ds(j * tall, tall)], dst_ref=strip(r, j),
             send_sem=dn_send.at[0, j], recv_sem=dn_recv.at[0, j],
             device_id=(r - 1, c, p), device_id_type=MESH)
+
+    def cut():
+        here = pl.ds((pieces - 1) * tall, tall - LENT)
+        return pltpu.make_async_remote_copy(
+            src_ref=b_hbm.at[here], dst_ref=b_all.at[1, here],
+            send_sem=dn_send.at[0, pieces - 1], recv_sem=dn_recv.at[0, pieces - 1],
+            device_id=(0, c, p), device_id_type=MESH)
+
+    def lend(core):
+        return pltpu.make_async_remote_copy(
+            src_ref=b_hbm.at[pl.ds(first, LENT)], dst_ref=lent.at[core],
+            send_sem=lend_send, recv_sem=lend_recv.at[core],
+            device_id=(1, HELPER, 1), device_id_type=MESH)
+
+    def pass_on(core):
+        return pltpu.make_async_remote_copy(
+            src_ref=lent.at[core], dst_ref=b_all.at[1, pl.ds(first, LENT)],
+            send_sem=pass_send.at[core], recv_sem=pass_recv,
+            device_id=(0, 0, core), device_id_type=MESH)
 
     def domains():
         return pltpu.make_async_remote_copy(
@@ -140,8 +155,8 @@
             across(d, e, h).start()
         sibling(d, h).start()
 
-    def mask(block, j, domain):
-        for t in range(j * tall // TILE, (j + 1) * tall // TILE):
+    def mask(block, start, end, domain):
+        for t in range(start // TILE, end // TILE):
             here = pl.ds(t * TILE, TILE)
             b_all[block, here, :] = b_all[block, here, :] * domain[t:t + 1, :].astype(jnp.bfloat16)
 
@@ -149,31 +164,50 @@
     def _():
         raw(0).start()
         domains().start()
-        for j in range(1, pieces):
+        for j in range(1, pieces - 1):
             raw(j).start()
+
+    @pl.when(giver)
+    def _():
+        cut().start()
+
+    @pl.when((r == 1) & (c > 0))
+    def _():
+        raw(pieces - 1).start()
+
+    @pl.when(r > 0)
+    def _():
+        pl.semaphore_signal(above_in, inc=1, device_id=(r - 1, c, p), device_id_type=MESH)
+
+    @pl.when(p == 1)
+    def _():
+        for e in bits:
+            pl.semaphore_signal(plane_in, inc=1, device_id=(r, others[e], p), device_id_type=MESH)
 
     loads[0].wait()
     loads[1].wait()
     for j in range(pieces):
-        mask(r, j, dm_ref)
+        mask(r, j * tall, (j + 1) * tall, dm_ref)
 
         @pl.when(r > 1)
         def _():
             down(r, 0, j).start()
-
-    @pl.when((p == 0) & (r < R - 1))
-    def _():
-        pl.semaphore_wait(above_in, 1)
-
-    @pl.when(r < R - 1)
-    def _():
-        for j in range(pieces):
-            up(r, 0, j).start()
 
     @pl.when(p == 1)
     def _():
         pl.semaphore_wait(plane_in, len(bits))
         pl.semaphore_signal(go, inc=1, device_id=(r, c, q), device_id_type=MESH)
+
+    def rise():
+        @pl.when(r < R - 1)
+        def _():
+            pl.semaphore_wait(above_in, 1)
+            for j in range(pieces):
+                up(r, 0, j).start()
+
+    @pl.when(p == 0)
+    def _():
+        rise()
 
     loads[2].wait()
     loads[3].wait()
@@ -189,12 +223,20 @@
     def _():
         pl.semaphore_wait(go, 1)
 
+    @pl.when(giver)
+    def _():
+        lend(p).start()
+
     for h in (1, 0):
         for e in bits:
             g = h if 2 * e < C else 1 - h
             across(0, e, g).start()
     for h in range(2):
         sibling(0, h).start()
+
+    @pl.when(p == 1)
+    def _():
+        rise()
 
     loads[4].wait()
     loads[5].wait()
@@ -211,7 +253,13 @@
     def receive(s, j):
         above, below = r + s + 1, r - s - 1
 
-        @pl.when(above < R)
+        short = (s, j) == (0, pieces - 1)
+        if short:
+            @pl.when(taker)
+            def _():
+                cut().wait_recv()
+
+        @pl.when((above < R) & jnp.logical_not(taker) if short else above < R)
         def _():
             down(above, s, j).wait_recv()
 
@@ -219,12 +267,12 @@
             def _():
                 down(above, s + 1, j).start()
 
-            if s == 0:
-                @pl.when(r == 0)
-                def _():
-                    if j == 0:
-                        domains().wait_recv()
-                    mask(1, j, dm_above)
+        if s == 0:
+            @pl.when(r == 0)
+            def _():
+                if j == 0:
+                    domains().wait_recv()
+                mask(1, j * tall, min((j + 1) * tall, first), dm_above)
 
         @pl.when(below >= 0)
         def _():
@@ -252,21 +300,35 @@
     strips = [(s, j) for s in range(R - 1) for j in range(pieces)]
 
     def take(count):
-        for _ in range(count):
-            if len(strips) > SPLIT:
-                receive(*strips.pop(0))
+        for _ in range(min(count, len(strips) - pieces)):
+            receive(*strips.pop(0))
 
     near = [d for d in range(1, C) if d in bits]
-    take(2)
+    take(FIRST * SPLIT)
     for h in (1, 0):
         for d in near:
             arrives(d, h if 2 * d < C else 1 - h)
-        take(2)
+        if h:
+            @pl.when(helper)
+            def _():
+                for core in range(2):
+                    lend(core).wait_recv()
+                    pass_on(core).start()
+        take(SPLIT)
     for d in sorted(range(1, C), key=lambda d: d.bit_count()):
         if d not in near:
             for h in range(2):
                 arrives(d, h)
-    take(1)
+    take(len(strips))
+
+    @pl.when(taker)
+    def _():
+        pass_on(p).wait_recv()
+
+    @pl.when(r == 0)
+    def _():
+        mask(1, first, depth, dm_above)
+
     for d in range(C):
         for h in range(2):
             sibling(d, h, q).wait_recv()
@@ -280,50 +342,78 @@
             receive(*strips.pop(0))
         add(s, j)
 
-    s, j = whole[-1]
-    for i in range(SPLIT - 1):
-        receive(s, j * SPLIT + i)
-
-        @pl.when(r == 0)
-        def _():
-            acc[...] += product(R - 1, j, i, SPLIT)
-
-        @pl.when(r == R - 1)
-        def _():
-            acc[...] += product(0, j, i, SPLIT)
-
-    receive(s, pieces - 1)
-
-    @pl.when(r == 0)
-    def _():
-        acc[...] = (acc[...] + product(R - 1, j, SPLIT - 1, SPLIT)) * inv[...]
-
-    @pl.when(r == R - 1)
-    def _():
-        acc[...] = (acc[...] + product(0, j, SPLIT - 1, SPLIT)) * inv[...]
-
-    @pl.when((r > 0) & (r < R - 1))
-    def _():
-        acc[...] = acc[...] * inv[...]
-
     for d in range(C):
         for h in range(2):
             sibling(d, h).wait_send()
             for e in onward(d, h):
                 across(d, e, h).wait_send()
-    for s in range(R - 1):
+
+    @pl.when((r == 0) & (R > 1))
+    def _():
         for j in range(pieces):
-            @pl.when((r + s < R) & (r > 0))
-            def _():
-                down(r + s, s, j).wait_send()
-
-            @pl.when((r - s >= 0) & (r < R - 1))
-            def _():
-                up(r - s, s, j).wait_send()
-
-    @pl.when(r == 1)
-    def _():
-        domains().wait_send()
+            up(r, 0, j).wait_send()
+
+    @pl.when((r == R - 1) & (R > 1))
+    def _():
+        for j in range(pieces):
+            down(r, 0, j).wait_send()
+
+    def sent():
+        for s in range(R - 1):
+            for j in range(pieces):
+                short = (s, j) == (0, pieces - 1)
+
+                @pl.when((r + s < R) & (r > 0) & (jnp.logical_not(giver) if short else True))
+                def _():
+                    down(r + s, s, j).wait_send()
+
+                @pl.when((r - s >= 0) & (r < R - 1))
+                def _():
+                    up(r - s, s, j).wait_send()
+
+        @pl.when(r == 1)
+        def _():
+            domains().wait_send()
+
+        @pl.when(giver)
+        def _():
+            cut().wait_send()
+            lend(p).wait_send()
+
+        @pl.when(helper)
+        def _():
+            for core in range(2):
+                pass_on(core).wait_send()
+
+    s, j = whole[-1]
+    for i in range(SPLIT - 1):
+        receive(s, j * SPLIT + i)
+
+        @pl.when(r == 0)
+        def _():
+            acc[...] += product(R - 1, j, i, SPLIT)
+
+        @pl.when(r == R - 1)
+        def _():
+            acc[...] += product(0, j, i, SPLIT)
+
+    receive(s, pieces - 1)
+
+    @pl.when(r == 0)
+    def _():
+        acc[...] = (acc[...] + product(R - 1, j, SPLIT - 1, SPLIT)) * inv[...]
+
+    @pl.when(r == R - 1)
+    def _():
+        acc[...] = (acc[...] + product(0, j, SPLIT - 1, SPLIT)) * inv[...]
+
+    @pl.when((r > 0) & (r < R - 1))
+    def _():
+        acc[...] = acc[...] * inv[...]
+
+    @pl.when((r > 0) & (r < R - 1))
+    def _():
+        sent()
 
 
 def solution(mesh):
@@ -353,7 +443,7 @@
                 pltpu.VMEM((1, cols), jnp.float32),
                 dma((6,)), dma((C, 2)), dma((C, 2)), dma((C, 2)), dma((C, 2)),
                 dma((R - 1, pieces)), dma((R - 1, pieces)), dma((R - 1, pieces)), dma((R - 1, pieces)),
-                dma, dma,
+                dma, dma, pltpu.VMEM((2, LENT, cols), jnp.bfloat16), dma, dma((2,)), dma((2,)), dma,
                 pltpu.SemaphoreType.REGULAR, pltpu.SemaphoreType.REGULAR, pltpu.SemaphoreType.REGULAR,
             ],
             compiler_params=pltpu.CompilerParams(

time: 23.6 us -> 23.2 us (0.983)
  Pallas kernels: 22.6 us -> 22.2 us
    pallas_call x1, Pallas kernels: 22.6 us -> 22.2 us  [local(): pl.pallas_call(functools.partial(kernel, R, C), out_shape=pltpu.VMEM((row...]
where the time goes in v3:
time: 23.2 us; the launch traced here: 23 us
  Pallas kernels  22.2 us (96%)
  local copies, waits for them, and re-layouts  0.8 us (3%)
    pallas_call x1, Pallas kernels, local(): pl.pallas_call(functools.partial(kernel, R, C), out_shape=pltpu.VMEM((row...  22.2 us
    unnamed x1, local copies, waits for them, and re-layouts  0.8 us

profile of v3, /device:TPU:0, one launch (start us, length us, event | category | flops | bytes accessed | tf_op | source)
XLA Modules:
  0.0 23.0 jit_solution(9275856393656266933)
XLA Ops:
  0.0 22.2 %shard_map.64 = f32[512,256]{1,0:T(8,128)S(1)} custom-call(bf16[512,256]{1,0:T(8,128)(2,1)} %a_hbm.1, s32[4,8]{1,0:T(4,128)} %bitcast.3, bf16[512,256]{1,0:T(8,128)(2,1)} %b_hbm.1, s32[8,256]{1,0:T(8,128)} %dm_hbm.1, f32[1,512]{1,0:T(1,128)} %bitcast.4, f32[1,256]{1,0:T(1,128)} %bitcast.5), custom_call_target="tpu_custom_call" | custom-call | flops 536870912 | bytes 4194304 | tf_op jit(solution)/shard_map/pallas_call | solution.py:430
  22.2 0.8 %copy.8 = f32[512,256]{1,0:T(8,128)} copy(f32[512,256]{1,0:T(8,128)S(1)} %shard_map.64) | data formatting | bytes 1048576

commit v4 on v3

--- a/solution.py
+++ b/solution.py
@@ -24,10 +24,22 @@
     return out
 
 
+def arrivals(R, pieces):
+    place, count = {}, 0
+    for s in range(R - 1):
+        own = list(range(pieces)) if s < R - 2 else [0] * (pieces - 1) + [1]
+        for upward in (0, 1):
+            if upward and 2 * s + 2 > R - 1:
+                count -= own[-1] + 1
+            for j in range(pieces):
+                place[upward, s, j] = count + own[j]
+            count += own[-1] + 1
+    return place, count
+
+
 def kernel(R, C, a_hbm, im_hbm, b_hbm, dm_hbm, v_hbm, o_hbm, acc,
-           a_all, b_all, inv, im_ref, dm_ref, dm_above, v_ref, o_ref, load_sem,
-           a_send, a_recv, sib_send, sib_recv, dn_send, dn_recv, up_send, up_recv, dm_send, dm_recv,
-           lent, lend_send, lend_recv, pass_send, pass_recv, above_in, plane_in, go):
+           a_all, b_all, inv, im_ref, dm_ref, dm_above, v_ref, o_ref,
+           lent, load_sem, a_sent, a_recv, sib_recv, b_sent, b_recv, dm_recv, above_in, plane_in):
     r, c, p = lax.axis_index("row"), lax.axis_index("col"), lax.axis_index("pair")
     q = 1 - p
     me = c * 2 + p
@@ -37,10 +49,11 @@
     pieces = parts * SPLIT
     tall = depth // pieces
     half = rows // 2
+    place, _ = arrivals(R, pieces)
     bits = [1 << i for i in range(C.bit_length() - 1)]
     others = [flipped(c, d, C) for d in range(C)]
     first = depth - LENT
-    giver, taker = (r == 1) & (c == 0), (r == 0) & (c == 0)
+    giver = (r == 1) & (c == 0)
     helper = (r == 1) & (c == HELPER) & (p == 1)
 
     loads = [
@@ -84,58 +97,62 @@
     def down(block, s, j):
         return pltpu.make_async_remote_copy(
             src_ref=strip(block, j), dst_ref=strip(block, j),
-            send_sem=dn_send.at[s, j], recv_sem=dn_recv.at[s, j],
+            send_sem=b_sent, recv_sem=b_recv.at[place[0, s, j]],
             device_id=(r - 1, c, p), device_id_type=MESH)
 
     def up(block, s, j):
         return pltpu.make_async_remote_copy(
             src_ref=strip(block, j), dst_ref=strip(block, j),
-            send_sem=up_send.at[s, j], recv_sem=up_recv.at[s, j],
+            send_sem=b_sent, recv_sem=b_recv.at[place[1, s, j]],
             device_id=(r + 1, c, p), device_id_type=MESH)
 
     def raw(j):
         return pltpu.make_async_remote_copy(
             src_ref=b_hbm.at[pl.ds(j * tall, tall)], dst_ref=strip(r, j),
-            send_sem=dn_send.at[0, j], recv_sem=dn_recv.at[0, j],
+            send_sem=b_sent, recv_sem=b_recv.at[place[0, 0, j]],
             device_id=(r - 1, c, p), device_id_type=MESH)
 
     def cut():
         here = pl.ds((pieces - 1) * tall, tall - LENT)
         return pltpu.make_async_remote_copy(
             src_ref=b_hbm.at[here], dst_ref=b_all.at[1, here],
-            send_sem=dn_send.at[0, pieces - 1], recv_sem=dn_recv.at[0, pieces - 1],
+            send_sem=b_sent, recv_sem=b_recv.at[place[0, 0, pieces - 1]],
             device_id=(0, c, p), device_id_type=MESH)
 
     def lend(core):
         return pltpu.make_async_remote_copy(
             src_ref=b_hbm.at[pl.ds(first, LENT)], dst_ref=lent.at[core],
-            send_sem=lend_send, recv_sem=lend_recv.at[core],
+            send_sem=b_sent, recv_sem=a_recv.at[0, core],
             device_id=(1, HELPER, 1), device_id_type=MESH)
 
     def pass_on(core):
         return pltpu.make_async_remote_copy(
             src_ref=lent.at[core], dst_ref=b_all.at[1, pl.ds(first, LENT)],
-            send_sem=pass_send.at[core], recv_sem=pass_recv,
+            send_sem=load_sem.at[1], recv_sem=b_recv.at[place[0, 0, pieces - 1]],
             device_id=(0, 0, core), device_id_type=MESH)
 
     def domains():
         return pltpu.make_async_remote_copy(
-            src_ref=dm_hbm, dst_ref=dm_above, send_sem=dm_send, recv_sem=dm_recv,
+            src_ref=dm_ref, dst_ref=dm_above, send_sem=load_sem.at[0], recv_sem=dm_recv,
             device_id=(r - 1, c, p), device_id_type=MESH)
 
     def across(d, e, h):
         piece = a_all.at[others[d] * 2 + p, pl.ds(h * half, half)]
         return pltpu.make_async_remote_copy(
             src_ref=piece, dst_ref=piece,
-            send_sem=a_send.at[d + e, h], recv_sem=a_recv.at[d + e, h],
+            send_sem=a_sent, recv_sem=a_recv.at[d + e, h],
             device_id=(r, others[e], p), device_id_type=MESH)
 
-    def sibling(d, h, core=None):
-        piece = a_all.at[others[d] * 2 + (p if core is None else core), pl.ds(h * half, half)]
+    def sibling(d, h):
+        piece = a_all.at[others[d] * 2 + p, pl.ds(h * half, half)]
         return pltpu.make_async_remote_copy(
             src_ref=piece, dst_ref=piece,
-            send_sem=sib_send.at[d, h], recv_sem=sib_recv.at[d, h],
+            send_sem=a_sent, recv_sem=sib_recv,
             device_id=(r, c, q), device_id_type=MESH)
+
+    def await_blocks(count, sem):
+        blocks = a_all.at[pl.ds(0, count)]
+        pltpu.make_async_copy(blocks, blocks, sem).wait()
 
     def onward(d, h):
         if d == 0:
@@ -149,7 +166,7 @@
         piece = a_all.at[others[d] * 2 + p, pl.ds(h * half, half)]
         pltpu.make_async_remote_copy(
             src_ref=piece, dst_ref=piece,
-            send_sem=a_send.at[d, h], recv_sem=a_recv.at[d, h],
+            send_sem=a_sent, recv_sem=a_recv.at[d, h],
             device_id=(r, others[e], p), device_id_type=MESH).wait_recv()
         for e in onward(d, h):
             across(d, e, h).start()
@@ -162,9 +179,7 @@
 
     @pl.when(r == 1)
     def _():
-        raw(0).start()
-        domains().start()
-        for j in range(1, pieces - 1):
+        for j in range(pieces - 1):
             raw(j).start()
 
     @pl.when(giver)
@@ -186,6 +201,11 @@
 
     loads[0].wait()
     loads[1].wait()
+
+    @pl.when(r == 1)
+    def _():
+        domains().start()
+
     for j in range(pieces):
         mask(r, j * tall, (j + 1) * tall, dm_ref)
 
@@ -196,7 +216,7 @@
     @pl.when(p == 1)
     def _():
         pl.semaphore_wait(plane_in, len(bits))
-        pl.semaphore_signal(go, inc=1, device_id=(r, c, q), device_id_type=MESH)
+        pl.semaphore_signal(plane_in, inc=1, device_id=(r, c, q), device_id_type=MESH)
 
     def rise():
         @pl.when(r < R - 1)
@@ -221,7 +241,7 @@
 
     @pl.when(p == 0)
     def _():
-        pl.semaphore_wait(go, 1)
+        pl.semaphore_wait(plane_in, 1)
 
     @pl.when(giver)
     def _():
@@ -253,39 +273,35 @@
     def receive(s, j):
         above, below = r + s + 1, r - s - 1
 
-        short = (s, j) == (0, pieces - 1)
-        if short:
-            @pl.when(taker)
-            def _():
-                cut().wait_recv()
-
-        @pl.when((above < R) & jnp.logical_not(taker) if short else above < R)
+        late = (s, j) == (0, pieces - 1)
+
+        @pl.when((above < R) & (r > 0) if late else above < R)
         def _():
             down(above, s, j).wait_recv()
 
-            @pl.when(r > 0)
-            def _():
-                down(above, s + 1, j).start()
-
-        if s == 0:
+            if s < R - 2:
+                @pl.when(r > 0)
+                def _():
+                    down(above, s + 1, j).start()
+
+        if s == 0 and not late:
             @pl.when(r == 0)
             def _():
                 if j == 0:
                     domains().wait_recv()
-                mask(1, j * tall, min((j + 1) * tall, first), dm_above)
+                mask(1, j * tall, (j + 1) * tall, dm_above)
 
         @pl.when(below >= 0)
         def _():
             up(below, s, j).wait_recv()
 
-            @pl.when(r < R - 1)
-            def _():
-                up(below, s + 1, j).start()
-
-    def product(block, j, part=0, of=1):
-        deep = width // of
-        k = pl.ds(j * width + part * deep, deep)
-        return jnp.dot(a_all[block * parts + j, :, part * deep:(part + 1) * deep], b_all[block, k, :],
+            if s < R - 2:
+                @pl.when(r < R - 1)
+                def _():
+                    up(below, s + 1, j).start()
+
+    def product(block, j):
+        return jnp.dot(a_all[block * parts + j], b_all[block, pl.ds(j * width, width), :],
                        preferred_element_type=jnp.float32)
 
     def add(s, j):
@@ -297,10 +313,10 @@
         def _():
             acc[...] += product(r - s - 1, j)
 
-    strips = [(s, j) for s in range(R - 1) for j in range(pieces)]
+    strips = [(s, j) for s in range(R - 2) for j in range(pieces)]
 
     def take(count):
-        for _ in range(min(count, len(strips) - pieces)):
+        for _ in range(min(count, len(strips))):
             receive(*strips.pop(0))
 
     near = [d for d in range(1, C) if d in bits]
@@ -321,99 +337,75 @@
                 arrives(d, h)
     take(len(strips))
 
-    @pl.when(taker)
-    def _():
-        pass_on(p).wait_recv()
-
     @pl.when(r == 0)
     def _():
-        mask(1, first, depth, dm_above)
-
-    for d in range(C):
-        for h in range(2):
-            sibling(d, h, q).wait_recv()
+        down(1, 0, pieces - 1).wait_recv()
+        mask(1, (pieces - 1) * tall, depth, dm_above)
+
+    await_blocks(C, sib_recv)
 
     acc[...] = product(r, 0)
     for j in range(1, parts):
         acc[...] += product(r, j)
-    whole = [(s, j) for s in range(R - 1) for j in range(parts)]
-    for s, j in whole[:-1]:
-        while strips and strips[0] <= (s, (j + 1) * SPLIT - 1):
-            receive(*strips.pop(0))
-        add(s, j)
-
-    for d in range(C):
-        for h in range(2):
-            sibling(d, h).wait_send()
-            for e in onward(d, h):
-                across(d, e, h).wait_send()
-
-    @pl.when((r == 0) & (R > 1))
-    def _():
-        for j in range(pieces):
-            up(r, 0, j).wait_send()
-
-    @pl.when((r == R - 1) & (R > 1))
-    def _():
-        for j in range(pieces):
-            down(r, 0, j).wait_send()
-
-    def sent():
-        for s in range(R - 1):
-            for j in range(pieces):
-                short = (s, j) == (0, pieces - 1)
-
-                @pl.when((r + s < R) & (r > 0) & (jnp.logical_not(giver) if short else True))
-                def _():
-                    down(r + s, s, j).wait_send()
-
-                @pl.when((r - s >= 0) & (r < R - 1))
-                def _():
-                    up(r - s, s, j).wait_send()
-
-        @pl.when(r == 1)
-        def _():
-            domains().wait_send()
-
-        @pl.when(giver)
-        def _():
-            cut().wait_send()
-            lend(p).wait_send()
-
-        @pl.when(helper)
-        def _():
-            for core in range(2):
-                pass_on(core).wait_send()
-
-    s, j = whole[-1]
-    for i in range(SPLIT - 1):
-        receive(s, j * SPLIT + i)
-
-        @pl.when(r == 0)
-        def _():
-            acc[...] += product(R - 1, j, i, SPLIT)
-
-        @pl.when(r == R - 1)
-        def _():
-            acc[...] += product(0, j, i, SPLIT)
-
-    receive(s, pieces - 1)
+    for s in range(R - 2):
+        for j in range(parts):
+            add(s, j)
+
+    def most(block):
+        for j in range(parts - 1):
+            acc[...] += product(block, j)
+        k = (parts - 1) * width
+        if SPLIT > 1:
+            acc[...] += jnp.dot(a_all[block * parts + parts - 1, :, :width - tall], b_all[block, k:depth - tall, :],
+                                preferred_element_type=jnp.float32)
+
+    def strips_of(block):
+        return b_all.at[block, pl.ds(0, depth - tall)]
 
     @pl.when(r == 0)
     def _():
-        acc[...] = (acc[...] + product(R - 1, j, SPLIT - 1, SPLIT)) * inv[...]
+        pltpu.make_async_copy(strips_of(R - 1), strips_of(R - 1), b_recv.at[place[0, R - 2, 0]]).wait()
+        most(R - 1)
 
     @pl.when(r == R - 1)
     def _():
-        acc[...] = (acc[...] + product(0, j, SPLIT - 1, SPLIT)) * inv[...]
+        pltpu.make_async_copy(strips_of(0), strips_of(0), b_recv.at[place[1, R - 2, 0]]).wait()
+        most(0)
+
+    await_blocks(2 * C - 1, a_sent)
+
+    @pl.when((r == 0) | (r == R - 1))
+    def _():
+        await_blocks(1, b_sent)
+
+    receive(R - 2, pieces - 1)
+
+    def finish(block):
+        k = (pieces - 1) * tall
+        last = jnp.dot(a_all[block * parts + parts - 1, :, width - tall:], b_all[block, k:k + tall, :],
+                       preferred_element_type=jnp.float32)
+        acc[...] = (acc[...] + last) * inv[...]
+
+    @pl.when(r == 0)
+    def _():
+        finish(R - 1)
+
+    @pl.when(r == R - 1)
+    def _():
+        finish(0)
 
     @pl.when((r > 0) & (r < R - 1))
     def _():
         acc[...] = acc[...] * inv[...]
-
-    @pl.when((r > 0) & (r < R - 1))
-    def _():
-        sent()
+        await_blocks(R + 1, b_sent)
+
+    @pl.when(r == 1)
+    def _():
+        domains().wait_send()
+
+    @pl.when(helper)
+    def _():
+        pltpu.make_async_copy(lent, lent, load_sem.at[1]).wait()
 
 
 def solution(mesh):
@@ -441,10 +433,9 @@
                 pltpu.VMEM(domain_mask.shape, jnp.int32),
                 pltpu.VMEM((1, rows), jnp.float32),
                 pltpu.VMEM((1, cols), jnp.float32),
-                dma((6,)), dma((C, 2)), dma((C, 2)), dma((C, 2)), dma((C, 2)),
-                dma((R - 1, pieces)), dma((R - 1, pieces)), dma((R - 1, pieces)), dma((R - 1, pieces)),
-                dma, dma, pltpu.VMEM((2, LENT, cols), jnp.bfloat16), dma, dma((2,)), dma((2,)), dma,
-                pltpu.SemaphoreType.REGULAR, pltpu.SemaphoreType.REGULAR, pltpu.SemaphoreType.REGULAR,
+                pltpu.VMEM((2, LENT, cols), jnp.bfloat16),
+                dma((6,)), dma, dma((C, 2)), dma, dma, dma((arrivals(R, pieces)[1],)), dma,
+                pltpu.SemaphoreType.REGULAR, pltpu.SemaphoreType.REGULAR,
             ],
             compiler_params=pltpu.CompilerParams(
                 collective_id=0, has_side_effects=True, vmem_limit_bytes=32 * 2**20),

time: 23.2 us -> 22.7 us (0.978)
  Pallas kernels: 22.2 us -> 21.7 us
    pallas_call x1, Pallas kernels: 22.2 us -> 21.7 us  [local(): pl.pallas_call(functools.partial(kernel, R, C), out_shape=pltpu.VMEM((row...]
where the time goes in v4:
time: 22.7 us; the launch traced here: 22.5 us
  Pallas kernels  21.7 us (96%)
  local copies, waits for them, and re-layouts  0.8 us (4%)
    pallas_call x1, Pallas kernels, local(): pl.pallas_call(functools.partial(kernel, R, C), out_shape=pltpu.VMEM((row...  21.7 us
    unnamed x1, local copies, waits for them, and re-layouts  0.8 us

profile of v4, /device:TPU:0, one launch (start us, length us, event | category | flops | bytes accessed | tf_op | source)
XLA Modules:
  0.0 22.5 jit_solution(15586945058323256007)
XLA Ops:
  0.0 21.7 %shard_map.64 = f32[512,256]{1,0:T(8,128)S(1)} custom-call(bf16[512,256]{1,0:T(8,128)(2,1)} %a_hbm.1, s32[4,8]{1,0:T(4,128)} %bitcast.3, bf16[512,256]{1,0:T(8,128)(2,1)} %b_hbm.1, s32[8,256]{1,0:T(8,128)} %dm_hbm.1, f32[1,512]{1,0:T(1,128)} %bitcast.4, f32[1,256]{1,0:T(1,128)} %bitcast.5), custom_call_target="tpu_custom_call" | custom-call | flops 536870912 | bytes 4194304 | tf_op jit(solution)/shard_map/pallas_call | solution.py:422
  21.7 0.8 %copy.8 = f32[512,256]{1,0:T(8,128)} copy(f32[512,256]{1,0:T(8,128)S(1)} %shard_map.64) | data formatting | bytes 1048576

commit v5 on v4

--- a/solution.py
+++ b/solution.py
@@ -8,10 +8,10 @@
 from jax.sharding import PartitionSpec as P
 
 TILE = 64
-SPLIT = 2
-FIRST = 1
-LENT = 64
+STRIPS = 4
+LENT = (96, 32)
 HELPER = 3
+LAG = 2
 MESH = pl.DeviceIdType.MESH
 
 
@@ -24,40 +24,47 @@
     return out
 
 
-def arrivals(R, pieces):
+def passes(C, d, h):
+    bits = [1 << i for i in range(C.bit_length() - 1)]
+    low, high = d & -d, 1 << (d.bit_length() - 1)
+    return [e for e in bits if d == 0 or (e < low if h == 0 else e > high)]
+
+
+def arrivals(R):
     place, count = {}, 0
     for s in range(R - 1):
-        own = list(range(pieces)) if s < R - 2 else [0] * (pieces - 1) + [1]
+        own = list(range(STRIPS)) if s < R - 2 else [0] * (STRIPS - 1) + [1]
         for upward in (0, 1):
             if upward and 2 * s + 2 > R - 1:
                 count -= own[-1] + 1
-            for j in range(pieces):
+            for j in range(STRIPS):
                 place[upward, s, j] = count + own[j]
             count += own[-1] + 1
     return place, count
 
 
 def kernel(R, C, a_hbm, im_hbm, b_hbm, dm_hbm, v_hbm, o_hbm, acc,
-           a_all, b_all, inv, im_ref, dm_ref, dm_above, v_ref, o_ref,
-           lent, load_sem, a_sent, a_recv, sib_recv, b_sent, b_recv, dm_recv, above_in, plane_in):
+           a_all, b_all, inv, im_ref, dm_ref, dm_above, energy,
+           lent, load_sem, a_sent, a_recv, lent_in, sib_recv, b_sent, b_recv, dm_recv, above_in, plane_in):
     r, c, p = lax.axis_index("row"), lax.axis_index("col"), lax.axis_index("pair")
     q = 1 - p
     me = c * 2 + p
     rows, width = a_hbm.shape
     depth, cols = b_hbm.shape
     parts = depth // width
-    pieces = parts * SPLIT
-    tall = depth // pieces
+    tall = depth // 4
+    spans = [pl.ds(j * tall, tall) for j in range(STRIPS)]
+    last = STRIPS - 1
     half = rows // 2
-    place, _ = arrivals(R, pieces)
+    place, _ = arrivals(R)
+    v_ref, o_ref = energy.at[:, pl.ds(0, rows)], energy.at[:, pl.ds(rows, cols)]
     bits = [1 << i for i in range(C.bit_length() - 1)]
     others = [flipped(c, d, C) for d in range(C)]
-    first = depth - LENT
     giver = (r == 1) & (c == 0)
     helper = (r == 1) & (c == HELPER) & (p == 1)
 
     loads = [
-        pltpu.make_async_copy(src, dst, load_sem.at[i]) for i, (src, dst) in enumerate([
+        pltpu.make_async_copy(src, dst, load_sem.at[min(i, 4)]) for i, (src, dst) in enumerate([
             (dm_hbm, dm_ref), (b_hbm, b_all.at[r]), (im_hbm, im_ref), (a_hbm, a_all.at[me]),
             (v_hbm, v_ref), (o_hbm, o_ref)])
     ]
@@ -92,7 +99,7 @@
         pl.semaphore_wait(barrier, 1)
 
     def strip(block, j):
-        return b_all.at[block, pl.ds(j * tall, tall)]
+        return b_all.at[block, spans[j]]
 
     def down(block, s, j):
         return pltpu.make_async_remote_copy(
@@ -108,27 +115,29 @@
 
     def raw(j):
         return pltpu.make_async_remote_copy(
-            src_ref=b_hbm.at[pl.ds(j * tall, tall)], dst_ref=strip(r, j),
+            src_ref=b_hbm.at[spans[j]], dst_ref=strip(r, j),
             send_sem=b_sent, recv_sem=b_recv.at[place[0, 0, j]],
             device_id=(r - 1, c, p), device_id_type=MESH)
 
-    def cut():
-        here = pl.ds((pieces - 1) * tall, tall - LENT)
+    def cut(core):
+        here = pl.ds(depth - tall, tall - LENT[core])
         return pltpu.make_async_remote_copy(
             src_ref=b_hbm.at[here], dst_ref=b_all.at[1, here],
-            send_sem=b_sent, recv_sem=b_recv.at[place[0, 0, pieces - 1]],
+            send_sem=b_sent, recv_sem=b_recv.at[place[0, 0, last]],
             device_id=(0, c, p), device_id_type=MESH)
 
     def lend(core):
         return pltpu.make_async_remote_copy(
-            src_ref=b_hbm.at[pl.ds(first, LENT)], dst_ref=lent.at[core],
-            send_sem=b_sent, recv_sem=a_recv.at[0, core],
+            src_ref=b_hbm.at[pl.ds(depth - LENT[core], LENT[core])],
+            dst_ref=lent.at[pl.ds(core * LENT[0], LENT[core])],
+            send_sem=b_sent, recv_sem=lent_in,
             device_id=(1, HELPER, 1), device_id_type=MESH)
 
     def pass_on(core):
         return pltpu.make_async_remote_copy(
-            src_ref=lent.at[core], dst_ref=b_all.at[1, pl.ds(first, LENT)],
-            send_sem=load_sem.at[1], recv_sem=b_recv.at[place[0, 0, pieces - 1]],
+            src_ref=lent.at[pl.ds(core * LENT[0], LENT[core])],
+            dst_ref=b_all.at[1, pl.ds(depth - LENT[core], LENT[core])],
+            send_sem=load_sem.at[1], recv_sem=b_recv.at[place[0, 0, last]],
             device_id=(0, 0, core), device_id_type=MESH)
 
     def domains():
@@ -136,11 +145,20 @@
             src_ref=dm_ref, dst_ref=dm_above, send_sem=load_sem.at[0], recv_sem=dm_recv,
             device_id=(r - 1, c, p), device_id_type=MESH)
 
+    def onward(d, h):
+        return passes(C, d, h)
+
+    relayed = [(d, h) for d in range(1, C) for h in range(2) if onward(d, h)]
+    leaves = [(d, h) for d in range(1, C) for h in range(2) if not onward(d, h)]
+
+    def halves(d, h):
+        return 1 + relayed.index((d, h)) if onward(d, h) else 0
+
     def across(d, e, h):
         piece = a_all.at[others[d] * 2 + p, pl.ds(h * half, half)]
         return pltpu.make_async_remote_copy(
             src_ref=piece, dst_ref=piece,
-            send_sem=a_sent, recv_sem=a_recv.at[d + e, h],
+            send_sem=a_sent, recv_sem=a_recv.at[halves(d + e, h)],
             device_id=(r, others[e], p), device_id_type=MESH)
 
     def sibling(d, h):
@@ -153,12 +171,6 @@
     def await_blocks(count, sem):
         blocks = a_all.at[pl.ds(0, count)]
         pltpu.make_async_copy(blocks, blocks, sem).wait()
-
-    def onward(d, h):
-        if d == 0:
-            return bits
-        low, high = d & -d, 1 << (d.bit_length() - 1)
-        return [e for e in bits if (e < low if h == 0 else e > high)]
 
     def arrives(d, h):
         low, high = d & -d, 1 << (d.bit_length() - 1)
@@ -166,29 +178,30 @@
         piece = a_all.at[others[d] * 2 + p, pl.ds(h * half, half)]
         pltpu.make_async_remote_copy(
             src_ref=piece, dst_ref=piece,
-            send_sem=a_sent, recv_sem=a_recv.at[d, h],
+            send_sem=a_sent, recv_sem=a_recv.at[halves(d, h)],
             device_id=(r, others[e], p), device_id_type=MESH).wait_recv()
         for e in onward(d, h):
             across(d, e, h).start()
         sibling(d, h).start()
 
-    def mask(block, start, end, domain):
-        for t in range(start // TILE, end // TILE):
+    def mask(block, j, domain):
+        for t in range(spans[j].start // TILE, (spans[j].start + spans[j].size) // TILE):
             here = pl.ds(t * TILE, TILE)
             b_all[block, here, :] = b_all[block, here, :] * domain[t:t + 1, :].astype(jnp.bfloat16)
 
     @pl.when(r == 1)
     def _():
-        for j in range(pieces - 1):
+        for j in range(last):
             raw(j).start()
 
-    @pl.when(giver)
-    def _():
-        cut().start()
+    for core in range(2):
+        @pl.when(giver & (p == core))
+        def _():
+            cut(core).start()
 
     @pl.when((r == 1) & (c > 0))
     def _():
-        raw(pieces - 1).start()
+        raw(last).start()
 
     @pl.when(r > 0)
     def _():
@@ -206,8 +219,8 @@
     def _():
         domains().start()
 
-    for j in range(pieces):
-        mask(r, j * tall, (j + 1) * tall, dm_ref)
+    for j in range(STRIPS):
+        mask(r, j, dm_ref)
 
         @pl.when(r > 1)
         def _():
@@ -222,7 +235,7 @@
         @pl.when(r < R - 1)
         def _():
             pl.semaphore_wait(above_in, 1)
-            for j in range(pieces):
+            for j in range(STRIPS):
                 up(r, 0, j).start()
 
     @pl.when(p == 0)
@@ -243,9 +256,10 @@
     def _():
         pl.semaphore_wait(plane_in, 1)
 
-    @pl.when(giver)
-    def _():
-        lend(p).start()
+    for core in range(2):
+        @pl.when(giver & (p == core))
+        def _():
+            lend(core).start()
 
     for h in (1, 0):
         for e in bits:
@@ -258,8 +272,7 @@
     def _():
         rise()
 
-    loads[4].wait()
-    loads[5].wait()
+    pltpu.make_async_copy(energy, energy, load_sem.at[4]).wait()
     for t in range(rows // 128):
         v = jnp.broadcast_to(v_ref[:, t * 128:(t + 1) * 128], (128, 128)).T
         for u in range(cols // 128):
@@ -270,10 +283,10 @@
                 keep = dm_ref[row:row + 1, lanes].astype(jnp.float32)
                 inv[pl.ds(row * TILE, TILE), lanes] = factor[w * TILE:(w + 1) * TILE] * keep
 
-    def receive(s, j):
-        above, below = r + s + 1, r - s - 1
-
-        late = (s, j) == (0, pieces - 1)
+    def from_above(s, j):
+        above = r + s + 1
+
+        late = (s, j) == (0, last)
 
         @pl.when((above < R) & (r > 0) if late else above < R)
         def _():
@@ -289,7 +302,10 @@
             def _():
                 if j == 0:
                     domains().wait_recv()
-                mask(1, j * tall, (j + 1) * tall, dm_above)
+                mask(1, j, dm_above)
+
+    def from_below(s, j):
+        below = r - s - 1
 
         @pl.when(below >= 0)
         def _():
@@ -313,34 +329,36 @@
         def _():
             acc[...] += product(r - s - 1, j)
 
-    strips = [(s, j) for s in range(R - 2) for j in range(pieces)]
+    each = [(s, j) for s in range(R - 2) for j in range(STRIPS)]
+    strips = sorted([(i, from_above, *x) for i, x in enumerate(each)] + [(i + LAG, from_below, *x) for i, x in enumerate(each)],
+                    key=lambda x: x[0])
 
     def take(count):
         for _ in range(min(count, len(strips))):
-            receive(*strips.pop(0))
-
-    near = [d for d in range(1, C) if d in bits]
-    take(FIRST * SPLIT)
-    for h in (1, 0):
-        for d in near:
-            arrives(d, h if 2 * d < C else 1 - h)
-        if h:
-            @pl.when(helper)
-            def _():
-                for core in range(2):
-                    lend(core).wait_recv()
-                    pass_on(core).start()
-        take(SPLIT)
-    for d in sorted(range(1, C), key=lambda d: d.bit_count()):
-        if d not in near:
-            for h in range(2):
-                arrives(d, h)
+            _, take_from, s, j = strips.pop(0)
+            take_from(s, j)
+
+    order = sorted(relayed, key=lambda x: (x[0].bit_count(), x[1] if 2 * x[0] >= C else 1 - x[1]))
+    take(6)
+    for d, h in order:
+        arrives(d, h)
+
+    @pl.when(helper)
+    def _():
+        pltpu.make_async_copy(lent, lent, lent_in).wait()
+        for core in range(2):
+            pass_on(core).start()
+
+    take(6)
+    await_blocks(len(leaves) // 2, a_recv.at[0])
+    for d, h in leaves:
+        sibling(d, h).start()
     take(len(strips))
 
     @pl.when(r == 0)
     def _():
-        down(1, 0, pieces - 1).wait_recv()
-        mask(1, (pieces - 1) * tall, depth, dm_above)
+        down(1, 0, last).wait_recv()
+        mask(1, last, dm_above)
 
     await_blocks(C, sib_recv)
 
@@ -355,7 +373,7 @@
         for j in range(parts - 1):
             acc[...] += product(block, j)
         k = (parts - 1) * width
-        if SPLIT > 1:
+        if tall < width:
             acc[...] += jnp.dot(a_all[block * parts + parts - 1, :, :width - tall], b_all[block, k:depth - tall, :],
                                 preferred_element_type=jnp.float32)
 
@@ -378,13 +396,14 @@
     def _():
         await_blocks(1, b_sent)
 
-    receive(R - 2, pieces - 1)
+    from_above(R - 2, last)
+    from_below(R - 2, last)
 
     def finish(block):
-        k = (pieces - 1) * tall
-        last = jnp.dot(a_all[block * parts + parts - 1, :, width - tall:], b_all[block, k:k + tall, :],
+        k = depth - tall
+        term = jnp.dot(a_all[block * parts + parts - 1, :, width - tall:], b_all[block, k:k + tall, :],
                        preferred_element_type=jnp.float32)
-        acc[...] = (acc[...] + last) * inv[...]
+        acc[...] = (acc[...] + term) * inv[...]
 
     @pl.when(r == 0)
     def _():
@@ -414,9 +433,9 @@
     def local(integrals, int_mask, amplitudes, domain_mask, virt_energy, occ_energy):
         rows, width = integrals.shape
         depth, cols = amplitudes.shape
-        pieces = depth // width * SPLIT
         hbm = pl.BlockSpec(memory_space=pl.ANY)
         dma = pltpu.SemaphoreType.DMA
+        relays = sum(bool(passes(C, d, h)) for d in range(1, C) for h in range(2))
         operands = (integrals, int_mask.T, amplitudes, domain_mask,
                     virt_energy.reshape(1, rows), occ_energy.reshape(1, cols))
         return pl.pallas_call(
@@ -431,10 +450,9 @@
                 pltpu.VMEM(int_mask.shape[::-1], jnp.int32),
                 pltpu.VMEM(domain_mask.shape, jnp.int32),
                 pltpu.VMEM(domain_mask.shape, jnp.int32),
-                pltpu.VMEM((1, rows), jnp.float32),
-                pltpu.VMEM((1, cols), jnp.float32),
-                pltpu.VMEM((2, LENT, cols), jnp.bfloat16),
-                dma((6,)), dma, dma((C, 2)), dma, dma, dma((arrivals(R, pieces)[1],)), dma,
+                pltpu.VMEM((1, rows + cols), jnp.float32),
+                pltpu.VMEM((sum(LENT), cols), jnp.bfloat16),
+                dma((5,)), dma, dma((1 + relays,)), dma, dma, dma, dma((arrivals(R)[1],)), dma,
                 pltpu.SemaphoreType.REGULAR, pltpu.SemaphoreType.REGULAR,
             ],
             compiler_params=pltpu.CompilerParams(

time: 22.7 us -> 22.6 us (level)
  no operation moved by 1% of the time
where the time goes in v5:
time: 22.6 us; the launch traced here: 22.4 us
  Pallas kernels  21.6 us (96%)
  local copies, waits for them, and re-layouts  0.8 us (4%)
    pallas_call x1, Pallas kernels, local(): pl.pallas_call(functools.partial(kernel, R, C), out_shape=pltpu.VMEM((row...  21.6 us
    unnamed x1, local copies, waits for them, and re-layouts  0.8 us

profile of v5, /device:TPU:0, one launch (start us, length us, event | category | flops | bytes accessed | tf_op | source)
XLA Modules:
  0.0 22.4 jit_solution(4495921211777255926)
XLA Ops:
  0.0 21.6 %shard_map.64 = f32[512,256]{1,0:T(8,128)S(1)} custom-call(bf16[512,256]{1,0:T(8,128)(2,1)} %a_hbm.1, s32[4,8]{1,0:T(4,128)} %bitcast.3, bf16[512,256]{1,0:T(8,128)(2,1)} %b_hbm.1, s32[8,256]{1,0:T(8,128)} %dm_hbm.1, f32[1,512]{1,0:T(1,128)} %bitcast.4, f32[1,256]{1,0:T(1,128)} %bitcast.5), custom_call_target="tpu_custom_call" | custom-call | flops 536870912 | bytes 4194304 | tf_op jit(solution)/shard_map/pallas_call | solution.py:441
  21.6 0.8 %copy.8 = f32[512,256]{1,0:T(8,128)} copy(f32[512,256]{1,0:T(8,128)S(1)} %shard_map.64) | data formatting | bytes 1048576

commit v6 on v5

--- a/solution.py
+++ b/solution.py
@@ -9,8 +9,8 @@
 
 TILE = 64
 STRIPS = 4
-LENT = (96, 32)
-HELPER = 3
+LENT = (112, 48)
+HELPERS = (3, 2)
 LAG = 2
 MESH = pl.DeviceIdType.MESH
 
@@ -61,7 +61,7 @@
     bits = [1 << i for i in range(C.bit_length() - 1)]
     others = [flipped(c, d, C) for d in range(C)]
     giver = (r == 1) & (c == 0)
-    helper = (r == 1) & (c == HELPER) & (p == 1)
+    helper = [(r == 1) & (c == HELPERS[core]) & (p == 1 - core) for core in range(2)]
 
     loads = [
         pltpu.make_async_copy(src, dst, load_sem.at[min(i, 4)]) for i, (src, dst) in enumerate([
@@ -131,7 +131,7 @@
             src_ref=b_hbm.at[pl.ds(depth - LENT[core], LENT[core])],
             dst_ref=lent.at[pl.ds(core * LENT[0], LENT[core])],
             send_sem=b_sent, recv_sem=lent_in,
-            device_id=(1, HELPER, 1), device_id_type=MESH)
+            device_id=(1, HELPERS[core], 1 - core), device_id_type=MESH)
 
     def pass_on(core):
         return pltpu.make_async_remote_copy(
@@ -343,10 +343,10 @@
     for d, h in order:
         arrives(d, h)
 
-    @pl.when(helper)
-    def _():
-        pltpu.make_async_copy(lent, lent, lent_in).wait()
-        for core in range(2):
+    for core in range(2):
+        @pl.when(helper[core])
+        def _():
+            lend(core).wait_recv()
             pass_on(core).start()
 
     take(6)
@@ -422,9 +422,10 @@
     def _():
         domains().wait_send()
 
-    @pl.when(helper)
-    def _():
-        pltpu.make_async_copy(lent, lent, load_sem.at[1]).wait()
+    for core in range(2):
+        @pl.when(helper[core])
+        def _():
+            pass_on(core).wait_send()
 
 
 def solution(mesh):

time: 22.6 us -> 22.5 us (level)
  no operation moved by 1% of the time
where the time goes in v6:
time: 22.5 us; the launch traced here: 22.2 us
  Pallas kernels  21.4 us (95%)
  local copies, waits for them, and re-layouts  0.8 us (4%)
    pallas_call x1, Pallas kernels, local(): pl.pallas_call(functools.partial(kernel, R, C), out_shape=pltpu.VMEM((row...  21.4 us
    unnamed x1, local copies, waits for them, and re-layouts  0.8 us

profile of v6, /device:TPU:0, one launch (start us, length us, event | category | flops | bytes accessed | tf_op | source)
XLA Modules:
  0.0 22.2 jit_solution(16786478205497630586)
XLA Ops:
  0.0 21.4 %shard_map.64 = f32[512,256]{1,0:T(8,128)S(1)} custom-call(bf16[512,256]{1,0:T(8,128)(2,1)} %a_hbm.1, s32[4,8]{1,0:T(4,128)} %bitcast.3, bf16[512,256]{1,0:T(8,128)(2,1)} %b_hbm.1, s32[8,256]{1,0:T(8,128)} %dm_hbm.1, f32[1,512]{1,0:T(1,128)} %bitcast.4, f32[1,256]{1,0:T(1,128)} %bitcast.5), custom_call_target="tpu_custom_call" | custom-call | flops 536870912 | bytes 4194304 | tf_op jit(solution)/shard_map/pallas_call | solution.py:442
  21.4 0.8 %copy.8 = f32[512,256]{1,0:T(8,128)} copy(f32[512,256]{1,0:T(8,128)S(1)} %shard_map.64) | data formatting | bytes 1048576

commit v7 on v6

--- a/solution.py
+++ b/solution.py
@@ -45,7 +45,7 @@
 
 def kernel(R, C, a_hbm, im_hbm, b_hbm, dm_hbm, v_hbm, o_hbm, acc,
            a_all, b_all, inv, im_ref, dm_ref, dm_above, energy,
-           lent, load_sem, a_sent, a_recv, lent_in, sib_recv, b_sent, b_recv, dm_recv, above_in, plane_in):
+           lent, load_sem, a_recv, lent_in, sib_recv, b_sent, b_recv, dm_recv, above_in, plane_in):
     r, c, p = lax.axis_index("row"), lax.axis_index("col"), lax.axis_index("pair")
     q = 1 - p
     me = c * 2 + p
@@ -158,14 +158,14 @@
         piece = a_all.at[others[d] * 2 + p, pl.ds(h * half, half)]
         return pltpu.make_async_remote_copy(
             src_ref=piece, dst_ref=piece,
-            send_sem=a_sent, recv_sem=a_recv.at[halves(d + e, h)],
+            send_sem=load_sem.at[3], recv_sem=a_recv.at[halves(d + e, h)],
             device_id=(r, others[e], p), device_id_type=MESH)
 
     def sibling(d, h):
         piece = a_all.at[others[d] * 2 + p, pl.ds(h * half, half)]
         return pltpu.make_async_remote_copy(
             src_ref=piece, dst_ref=piece,
-            send_sem=a_sent, recv_sem=sib_recv,
+            send_sem=load_sem.at[3], recv_sem=sib_recv,
             device_id=(r, c, q), device_id_type=MESH)
 
     def await_blocks(count, sem):
@@ -178,7 +178,7 @@
         piece = a_all.at[others[d] * 2 + p, pl.ds(h * half, half)]
         pltpu.make_async_remote_copy(
             src_ref=piece, dst_ref=piece,
-            send_sem=a_sent, recv_sem=a_recv.at[halves(d, h)],
+            send_sem=load_sem.at[3], recv_sem=a_recv.at[halves(d, h)],
             device_id=(r, others[e], p), device_id_type=MESH).wait_recv()
         for e in onward(d, h):
             across(d, e, h).start()
@@ -390,7 +390,7 @@
         pltpu.make_async_copy(strips_of(0), strips_of(0), b_recv.at[place[1, R - 2, 0]]).wait()
         most(0)
 
-    await_blocks(2 * C - 1, a_sent)
+    await_blocks(2 * C - 1, load_sem.at[3])
 
     @pl.when((r == 0) | (r == R - 1))
     def _():
@@ -453,7 +453,7 @@
                 pltpu.VMEM(domain_mask.shape, jnp.int32),
                 pltpu.VMEM((1, rows + cols), jnp.float32),
                 pltpu.VMEM((sum(LENT), cols), jnp.bfloat16),
-                dma((5,)), dma, dma((1 + relays,)), dma, dma, dma, dma((arrivals(R)[1],)), dma,
+                dma((5,)), dma((1 + relays,)), dma, dma, dma, dma((arrivals(R)[1],)), dma,
                 pltpu.SemaphoreType.REGULAR, pltpu.SemaphoreType.REGULAR,
             ],
             compiler_params=pltpu.CompilerParams(

time: 22.5 us -> 22.5 us (level)
  no operation moved by 1% of the time
where the time goes in v7:
time: 22.5 us; the launch traced here: 22.2 us
  Pallas kernels  21.4 us (95%)
  local copies, waits for them, and re-layouts  0.8 us (4%)
    pallas_call x1, Pallas kernels, local(): pl.pallas_call(functools.partial(kernel, R, C), out_shape=pltpu.VMEM((row...  21.4 us
    unnamed x1, local copies, waits for them, and re-layouts  0.8 us

profile of v7, /device:TPU:0, one launch (start us, length us, event | category | flops | bytes accessed | tf_op | source)
XLA Modules:
  0.0 22.2 jit_solution(14491538377471547530)
XLA Ops:
  0.0 21.4 %shard_map.64 = f32[512,256]{1,0:T(8,128)S(1)} custom-call(bf16[512,256]{1,0:T(8,128)(2,1)} %a_hbm.1, s32[4,8]{1,0:T(4,128)} %bitcast.3, bf16[512,256]{1,0:T(8,128)(2,1)} %b_hbm.1, s32[8,256]{1,0:T(8,128)} %dm_hbm.1, f32[1,512]{1,0:T(1,128)} %bitcast.4, f32[1,256]{1,0:T(1,128)} %bitcast.5), custom_call_target="tpu_custom_call" | custom-call | flops 536870912 | bytes 4194304 | tf_op jit(solution)/shard_map/pallas_call | solution.py:442
  21.4 0.8 %copy.8 = f32[512,256]{1,0:T(8,128)} copy(f32[512,256]{1,0:T(8,128)S(1)} %shard_map.64) | data formatting | bytes 1048576
